TPU v7x, 32 devices: a whole 2x2x4 slice. The times are simulated.
32 devices in a mesh: groups: 2 (over x), cols: 16 (over z, y, core).
Axes of the slice: x: 2, y: 2, z: 4, core: 2. Of those that a mesh axis runs over, the one named last changes fastest.
Arguments:
- state_field: bfloat16 [256, 256, 256], P(('groups', 'cols')), parts along dimension 0, may hold values from -6 to 6
- cotangent: bfloat16 [256, 256, 256], P(('groups', 'cols')), parts along dimension 0, may hold values from -6 to 6
- interp_blocks: bfloat16 [256, 7, 256, 256], P(('groups', 'cols')), parts along dimension 0, may hold values from -0.125 to 0.125
- upstream: int32 [256, 7], P(('groups', 'cols')), parts along dimension 0, may hold values from 0 to 127, as said below
- src_counts: int32 [256], P(('groups', 'cols')), parts along dimension 0, may hold values from 1 to 7, as said below
- w_in: bfloat16 [256, 512], replicated, may hold values from -0.375 to 0.375
- in_bias: float32 [512], replicated, may hold values from -4 to 4
- w_out: bfloat16 [512, 256], replicated, may hold values from -0.25 to 0.25
Outputs:
- grad_state: float32 [256, 256, 256], P(('groups', 'cols')), parts along dimension 0
- grad_w_in: float32 [512, 512], P('groups'), parts along dimension 0
- grad_w_out: float32 [1024, 256], P('groups'), parts along dimension 0
There are 2 independent parts, one for each index of `groups`. A program takes and returns all parts, laid end to end along the dimension named above; an argument that names none is the same for every part. Nothing has to cross between parts.
Inputs may be any that keep to these rules, and one draw needn't show every extreme that they name: `upstream`: each entry of row t lies within 8 tiles of t in the periodic order of tiles, between t - 8 and t + 8 modulo 128; in tile 0 the first slot names tile 8. Slots at or past the tile's count are unused. `src_counts`: tile 0 has 7 live slots.
All inputs are finite; a program needn't handle non-finite values.
Results may differ from a plain program's by a relative error of at most 0.0047.
Values may be sent and summed in bfloat16 or wider, within the bound.
A program may use at most 128 MiB of HBM per device.

v0:
```python
import jax
import jax.numpy as jnp
from jax import lax
from jax.sharding import PartitionSpec as P


def with_halo(array, sides, width):
    for axis, dim in sides:
        size, length = (lax.axis_size(axis), array.shape[dim])
        up = [(i, (i + 1) % size) for i in range(size)]
        down = [(j, i) for i, j in up]
        last = lax.slice_in_dim(array, length - width, length, axis=dim)
        initial = lax.slice_in_dim(array, 0, width, axis=dim)
        before = lax.ppermute(last, axis, up)
        after = lax.ppermute(initial, axis, down)
        array = jnp.concatenate([before, array, after], axis=dim)
    return array


def from_behind(array, axis, by):
    length = lax.axis_size(axis)
    return lax.ppermute(array, axis, [(i, (i + by) % length) for i in range(length)])


def per_device(state_field, cotangent, interp_blocks, upstream, src_counts, w_in, in_bias, w_out):
    tiles_dev = state_field.shape[0]
    tile_cols = state_field.shape[1]
    feat_dim = state_field.shape[2]
    slot_count = upstream.shape[1]
    col_count = lax.axis_size("cols")
    tile_total = tiles_dev * col_count
    position = lax.axis_index("cols")
    live_slot = jnp.arange(slot_count)[None, :] < src_counts[:, None]
    masked_blocks = interp_blocks * live_slot[:, :, None, None].astype(jnp.bfloat16)
    local_slot = (upstream - position * tiles_dev + tiles_dev) % tile_total
    near_tiles = with_halo(state_field, (("cols", 0),), tiles_dev)
    upstream_cells = jnp.take(near_tiles, local_slot.reshape(-1), axis=0)
    upstream_cells = upstream_cells.reshape(tiles_dev, slot_count, tile_cols, feat_dim)
    transported = jnp.einsum(
        "tkcd,tkdf->tcf", masked_blocks, upstream_cells, preferred_element_type=jnp.float32
    ).astype(jnp.bfloat16)
    col_rows = transported.reshape(tiles_dev * tile_cols, feat_dim)
    pre_act = jnp.dot(col_rows, w_in, preferred_element_type=jnp.float32) + in_bias
    sigmoid_val = jax.nn.sigmoid(pre_act)
    hidden = (pre_act * sigmoid_val).astype(jnp.bfloat16)
    cot_rows = cotangent.reshape(tiles_dev * tile_cols, feat_dim)
    back_grad = jnp.dot(cot_rows, w_out.T, preferred_element_type=jnp.float32)
    pre_grad = (back_grad * sigmoid_val * (1.0 + pre_act * (1.0 - sigmoid_val))).astype(
        jnp.bfloat16
    )
    upstream_grad = (
        cot_rows.astype(jnp.float32) + jnp.dot(pre_grad, w_in.T, preferred_element_type=jnp.float32)
    ).astype(jnp.bfloat16)
    grad_in_part = jnp.dot(col_rows.T, pre_grad, preferred_element_type=jnp.float32)
    grad_out_part = jnp.dot(hidden.T, cot_rows, preferred_element_type=jnp.float32)
    grad_w_in, grad_w_out = lax.psum((grad_in_part, grad_out_part), "cols")
    norm_scale = 1.0 / jnp.sqrt(jnp.float32(tile_total * tile_cols))
    grad_w_in = grad_w_in * norm_scale
    grad_w_out = grad_w_out * norm_scale
    upstream_grad = upstream_grad.reshape(tiles_dev, tile_cols, feat_dim)
    products = jnp.einsum(
        "tkcd,tcf->tkdf", masked_blocks, upstream_grad, preferred_element_type=jnp.float32
    )
    slot_table = (
        local_slot.reshape(-1)[None, :] == jnp.arange(3 * tiles_dev, dtype=jnp.int32)[:, None]
    ).astype(jnp.float32)
    contrib = jnp.einsum(
        "wp,pdf->wdf",
        slot_table,
        products.reshape(tiles_dev * slot_count, tile_cols, feat_dim),
        precision=lax.Precision.HIGHEST,
    )
    rounded = contrib.astype(jnp.bfloat16)
    left_part = from_behind(rounded[:tiles_dev], "cols", -1)
    right_part = from_behind(rounded[2 * tiles_dev :], "cols", 1)
    grad_state = (
        rounded[tiles_dev : 2 * tiles_dev].astype(jnp.float32)
        + left_part.astype(jnp.float32)
        + right_part.astype(jnp.float32)
    )
    return (grad_state, grad_w_in, grad_w_out)


def solution(mesh):
    placed = (
        P(("groups", "cols"), None, None),
        P(("groups", "cols"), None, None),
        P(("groups", "cols"), None, None, None),
        P(("groups", "cols"), None),
        P(("groups", "cols")),
        P(),
        P(),
        P(),
    )
    return jax.shard_map(
        per_device,
        mesh=mesh,
        in_specs=placed,
        out_specs=(P(("groups", "cols"), None, None), P("groups", None), P("groups", None)),
        check_vma=False,
    )
```

profile of v0, /device:TPU:1, one launch (start us, length us, event | category | flops | bytes accessed | tf_op | source)
XLA Modules:
  0.0 198.8 jit_solution(12337687888679165956)
XLA Ops:
  7.2 2.7 %collective-permute-start = (bf16[8,256,256]{2,1,0:T(8,128)(2,1)}, bf16[8,256,256]{2,1,0:T(8,128)(2,1)S(1)}, u32[]{:S(2)}, u32[]{:S(2)}) collective-permute-start(bf16[8,256,256]{2,1,0:T(8,128)(2,1)} %param.8), channel_id=1, source_target_pairs={{0,1},{1,2},{2,3},{3,4},{4,5},{5,6},{6,7},{7,8},{8,9},{9,10},{10,1... | collective-permute-start | bytes 3145736 | tf_op jit(solution)/shard_map/ppermute | solution.py:14
  9.9 0.7 compare_and_fusion
  10.8 0.7 fusion.24
  11.5 21.7 %collective-permute-done = bf16[8,256,256]{2,1,0:T(8,128)(2,1)S(1)} collective-permute-done((bf16[8,256,256]{2,1,0:T(8,128)(2,1)}, bf16[8,256,256]{2,1,0:T(8,128)(2,1)S(1)}, u32[]{:S(2)}, u32[]{:S(2)}) %collective-permute-start) | collective-permute-done | bytes 1048608 | tf_op jit(solution)/shard_map/ppermute | solution.py:14
  33.2 1.0 copy-done.6
  34.2 1.5 collective-permute-done.1
  35.7 2.0 %pad_maximum_fusion = bf16[24,256,256]{2,1,0:T(8,128)(2,1)S(1)} fusion(bf16[8,256,256]{2,1,0:T(8,128)(2,1)} %collective-permute-done.1, bf16[8,256,256]{2,1,0:T(8,128)(2,1)} %param.8, bf16[8,256,256]{2,1,0:T(8,128)(2,1)} %copy-done.6), kind=kLoop, calls=%fused_computation.15 | loop fusion | flops 3145728 | bytes 6291456 | tf_op jit(solution)/shard_map/concatenate | solution.py:16
  37.7 5.3 %gather_fusion = bf16[56,256,256]{2,1,0:T(8,128)(2,1)} fusion(bf16[24,256,256]{2,1,0:T(8,128)(2,1)S(1)} %pad_maximum_fusion, s32[1024]{0:T(1024)S(1)} %pad_clamp_fusion), kind=kCustom, calls=%fused_computation | custom fusion | bytes 14680288 | tf_op jit(solution)/shard_map/jit(_take)/gather | solution.py:37
  43.0 7.3 %bitcast_convert_fusion = bf16[8,256,256]{2,1,0:T(8,128)(2,1)S(1)} fusion(bf16[8,7,256,256]{3,2,1,0:T(8,128)(2,1)} %bitcast.31, pred[8,7]{1,0:T(8,128)(4,1)S(1)} %get-tuple-element.8, bf16[8,7,256,256]{3,2,1,0:T(8,128)(2,1)} %param.10, bf16[8,7]{1,0:T(8,128)(2,1)S(1)} %fusion.24), kind=kOutput, calls=%fused_computation.19 | convolution fusion | flops 1886912512 | bytes 15728808 | tf_op jit(solution)/shard_map/tkcd,tkdf->tcf/dot_general | solution.py:39
  50.4 0.7 fusion.29
  52.0 2.1 %fusion.15 = f32[512,256]{1,0:T(8,128)} fusion(bf16[2048,256]{1,0:T(8,128)(2,1)S(1)} %bitcast.34, f32[2048,512]{1,0:T(8,128)S(1)} %fusion.29, f32[512]{0:T(512)S(1)} %copy-done.8), kind=kOutput, calls=%fused_computation.21 | convolution fusion | flops 543162368 | bytes 5769216 | tf_op jit(solution)/shard_map/dot_general | solution.py:55
  54.0 1.9 multiply_convert_fusion.1
  56.0 1.3 copy-done.3
  57.3 0.7 fusion.11
  58.1 8.0 %fusion.5 = f32[8,7,256,256]{3,2,1,0:T(8,128)} fusion(bf16[8,256,256,1]{2,1,3,0:T(8,128)(2,1)S(1)} %bitcast.30, bf16[8,7,256,256]{3,2,1,0:T(8,128)(2,1)S(1)} %bitcast.29, bf16[8,7]{1,0:T(8,128)(2,1)S(1)} %fusion.24), kind=kOutput, calls=%fused_computation.6 | convolution fusion | flops 1882718208 | bytes 23068784 | tf_op jit(solution)/shard_map/tkcd,tcf->tkdf/dot_general | solution.py:61
  66.0 18.2 %fusion.12 = bf16[24,256,256]{2,0,1:T(8,128)(2,1)S(1)} fusion(f32[56,256,256]{2,1,0:T(8,128)} %bitcast.27, s32[56]{0:T(128)S(1)} %eq.17), kind=kOutput, calls=%fused_computation.18 | convolution fusion | flops 1058538816 | bytes 17826016 | tf_op jit(solution)/shard_map/wp,pdf->wdf/dot_general | solution.py:67
  84.3 1.5 fusion.28
  85.7 1.7 collective-permute-start.3
  87.5 1.5 fusion.30
  89.0 95.3 %all-reduce.3.cloned.1.call-done = (f32[256,512]{1,0:T(8,128)}, f32[512,256]{1,0:T(8,128)}) async-done(((f32[256,512]{1,0:T(8,128)}, f32[512,256]{1,0:T(8,128)}), (f32[256,512]{1,0:T(8,128)}, f32[512,256]{1,0:T(8,128)})) %all-reduce.3.cloned.1.call-update) | async-done | bytes 1048592 | tf_op jit(solution)/shard_map/psum | solution.py:56
  184.3 1.9 broadcast_multiply_fusion.1
  186.2 1.9 broadcast_multiply_fusion
  188.1 1.9 convert_add_fusion
  190.0 2.0 copy.13
  (31 shorter events, 1.1 us)
Async XLA Ops:
  7.2 43.2 %copy-start = (bf16[256,512]{1,0:T(8,128)(2,1)S(1)}, bf16[256,512]{1,0:T(8,128)(2,1)}, u32[]{:S(2)}) copy-start(bf16[256,512]{1,0:T(8,128)(2,1)} %param.13) | copy-start | bytes 786436
  7.2 177.1 %all-reduce.3.cloned.1.call-start = ((), (), s32[]{:S(2)}) async-start(), calls=%async_computation | async-start | bytes 2097152 | tf_op jit(solution)/shard_map/psum | solution.py:56
  7.2 26.0 %collective-permute-start = (bf16[8,256,256]{2,1,0:T(8,128)(2,1)}, bf16[8,256,256]{2,1,0:T(8,128)(2,1)S(1)}, u32[]{:S(2)}, u32[]{:S(2)}) collective-permute-start(bf16[8,256,256]{2,1,0:T(8,128)(2,1)} %param.8), channel_id=1, source_target_pairs={{0,1},{1,2},{2,3},{3,4},{4,5},{5,6},{6,7},{7,8},{8,9},{9,10},{10,1... | collective-permute-start | bytes 3145736 | tf_op jit(solution)/shard_map/ppermute | solution.py:14
  9.9 25.8 %collective-permute-start.1 = (bf16[8,256,256]{2,1,0:T(8,128)(2,1)}, bf16[8,256,256]{2,1,0:T(8,128)(2,1)}, u32[]{:S(2)}, u32[]{:S(2)}) collective-permute-start(bf16[8,256,256]{2,1,0:T(8,128)(2,1)} %param.8), channel_id=1, source_target_pairs={{1,0},{2,1},{3,2},{4,3},{5,4},{6,5},{7,6},{8,7},{9,8},{10,9},{11,1... | collective-permute-start | bytes 3145736 | tf_op jit(solution)/shard_map/ppermute | solution.py:15
  33.2 1.0 copy-start.6
  50.3 1.0 copy-start.1
  50.4 1.6 copy-start.5
  50.4 1.6 copy-start.8
  50.4 7.7 %slice-start = ((s8[7340032]{0:T(1024)(128)(4,1)}), s8[4194304]{0:T(1024)(128)(4,1)S(1)}, s32[]{:S(2)}) async-start(s8[7340032]{0:T(1024)(128)(4,1)} %bitcast.28), calls=%async_computation.1 | async-start | bytes 8388608
  52.0 2.1 %copy-start.7 = (bf16[512,256]{1,0:T(8,128)(2,1)S(1)}, bf16[512,256]{1,0:T(8,128)(2,1)}, u32[]{:S(2)}) copy-start(bf16[512,256]{1,0:T(8,128)(2,1)} %param.15) | copy-start | bytes 786436
  52.0 6.1 %slice-start.1 = ((s8[7340032]{0:T(1024)(128)(4,1)}), s8[3145728]{0:T(1024)(128)(4,1)S(1)}, s32[]{:S(2)}) async-start(s8[7340032]{0:T(1024)(128)(4,1)} %bitcast.28), calls=%async_computation.2 | async-start | bytes 6291456
  56.0 1.3 copy-start.3
  84.2 3.2 %copy-start.2 = (bf16[8,256,256]{2,1,0:T(8,128)(2,1)S(1)}, bf16[8,256,256]{2,1,0:T(8,128)(2,1)}, u32[]{:S(2)}) copy-start(bf16[8,256,256]{2,1,0:T(8,128)(2,1)} %copy-done.1) | copy-start | bytes 3145732
  84.2 3.2 %copy-start.4 = (bf16[2048,512]{1,0:T(8,128)(2,1)S(1)}, bf16[2048,512]{1,0:T(8,128)(2,1)}, u32[]{:S(2)}) copy-start(bf16[2048,512]{1,0:T(8,128)(2,1)} %copy-done.3) | copy-start | bytes 6291460
  85.7 102.4 %collective-permute-start.2 = (bf16[8,256,256]{2,0,1:T(8,128)(2,1)}, bf16[8,256,256]{2,0,1:T(8,128)(2,1)}, u32[]{:S(2)}, u32[]{:S(2)}) collective-permute-start(bf16[8,256,256]{2,0,1:T(8,128)(2,1)} %get-tuple-element.10), channel_id=1, source_target_pairs={{0,15},{1,0},{2,1},{3,2},{4,3},{5,4},{6,5},{7,6},{8,7},{9,8},{10,9... | collective-permute-start | bytes 3145736 | tf_op jit(solution)/shard_map/ppermute | solution.py:22
  85.7 102.4 %collective-permute-start.3 = (bf16[8,256,256]{2,0,1:T(8,128)(2,1)}, bf16[8,256,256]{2,0,1:T(8,128)(2,1)}, u32[]{:S(2)}, u32[]{:S(2)}) collective-permute-start(bf16[8,256,256]{2,0,1:T(8,128)(2,1)} %get-tuple-element.11), channel_id=1, source_target_pairs={{0,1},{1,2},{2,3},{3,4},{4,5},{5,6},{6,7},{7,8},{8,9},{9,10},{10,1... | collective-permute-start | bytes 3145736 | tf_op jit(solution)/shard_map/ppermute | solution.py:22
Sparse Core Ops, SparseCore 0:
  89.1 95.1 all-reduce.2
where the time goes:
time: 200 us; the launch traced here: 199 us
  waiting for transfers between devices  119 us (60%)
  matrix products  40.5 us (20%)
  between operations  14.2 us (7%)
  local copies, waits for them, and re-layouts  12 us (6%)
  other arithmetic  9.11 us (5%)
  starting transfers between devices  4.47 us (2%)
    psum x1, waiting for transfers between devices, per_device(): grad_w_in, grad_w_out = lax.psum((grad_in_part, grad_out_part), 'cols')  95.3 us
    ppermute x1, waiting for transfers between devices, with_halo(): before = lax.ppermute(last, axis, up)  21.7 us
    dot_general x1, matrix products, per_device(): jnp.einsum('wp,pdf->wdf', slot_table, products.reshape(tiles_dev * slot_c...  18.2 us
    dot_general x1, matrix products, per_device(): jnp.einsum('tkcd,tcf->tkdf', masked_blocks, upstream_grad, preferred_elem...  7.96 us
    dot_general x1, matrix products, per_device(): jnp.einsum('tkcd,tkdf->tcf', masked_blocks, upstream_cells, preferred_ele...  7.34 us
    gather x1, local copies, waits for them, and re-layouts, per_device(): upstream_cells = jnp.take(near_tiles, local_slot.reshape(-1), axis=0)  5.27 us
    unnamed x23, local copies, waits for them, and re-layouts  5.15 us
  transfers between devices with their start and end apart: 5, of which 3 were waited for; matrix products, arithmetic and copies ran while one was open for 3% of the time, Pallas kernels for 0%

commit v1 on v0

v1 whole, which is shorter than its diff:
```python
import functools

import jax
import jax.numpy as jnp
from jax import lax
from jax.experimental import pallas as pl
from jax.experimental.pallas import tpu as pltpu
from jax.sharding import PartitionSpec as P

F32 = jnp.float32
BF16 = jnp.bfloat16
MESH = pl.DeviceIdType.MESH
TN = (((0,), (0,)), ((), ()))
NT = (((1,), (1,)), ((), ()))


def mm(a, b):
    return jnp.dot(a, b, preferred_element_type=F32)


def kernel(
    n,
    table,
    state,
    cot_hbm,
    blocks_hbm,
    w_in,
    bias,
    w_out,
    out_state,
    out_w,
    near,
    land,
    blocks,
    cot,
    sums,
    xs,
    hs,
    pgs,
    far_out,
    sib_out,
    far_in,
    sib_in,
    out_buf,
    acc,
    core_in,
    z_out,
    z_in,
    y_out,
    y_in,
    gw,
    local_sem,
    blocks_sem,
    out_sem,
    far_ssem,
    far_rsem,
    sib_ssem,
    sib_rsem,
    cfar_ssem,
    cfar_rsem,
    csib_ssem,
    csib_rsem,
    core_sem,
    z_ssem,
    z_rsem,
    y_sem,
    g_ssem,
    g_rsem,
    last_sem,
):
    td, slots = blocks.shape[0], blocks.shape[1]
    nz = z_out.shape[0]
    rz = z_out.shape[1]
    pairs = td * slots
    me = lax.axis_index("cols")
    par = lax.rem(me, 2)
    sib = me + 1 - 2 * par
    far = lax.rem(me - 1 + 2 * par + n, n)
    zi = me // 4
    low = lax.rem(me, 4)
    y_mate = me + 2 - 4 * (low // 2)
    z_mates = [lax.rem(zi + d, nz) * 4 + low for d in range(1, nz)]

    def tile_at(s):
        return par * s + (1 - par) * (td - 1 - s)

    def send(src, dst, ssem, rsem, to):
        return pltpu.make_async_remote_copy(
            src_ref=src,
            dst_ref=dst,
            send_sem=ssem,
            recv_sem=rsem,
            device_id={"cols": to},
            device_id_type=MESH,
        )

    own_copy = pltpu.make_async_copy(state, near.at[pl.ds(td, td)], local_sem.at[0])
    own_copy.start()
    cot_copy = pltpu.make_async_copy(cot_hbm, cot, local_sem.at[1])
    cot_copy.start()

    def load_blocks(s):
        t = tile_at(s)
        return pltpu.make_async_copy(blocks_hbm.at[t], blocks.at[t], blocks_sem.at[s])

    for s in range(td):
        load_blocks(s).start()

    barrier = pltpu.get_barrier_semaphore()
    mates = [sib, far, y_mate] + z_mates
    for mate in mates:
        pl.semaphore_signal(barrier, inc=1, device_id={"cols": mate}, device_id_type=MESH)
    pl.semaphore_wait(barrier, len(mates))

    def far_state(s):
        t = tile_at(td - 1 - s)
        return send(state.at[t], land.at[s], far_ssem.at[s], far_rsem.at[s], far)

    for s in range(td):
        far_state(s).start()
    sib_state = send(state, near.at[pl.ds(2 * td * par, td)], sib_ssem, sib_rsem, sib)
    sib_state.start()

    near[3 * td] = jnp.zeros(near.shape[1:], BF16)
    sums[pairs] = jnp.zeros(sums.shape[1:], F32)
    own_copy.wait()
    cot_copy.wait()
    sib_state.wait()
    far_base = 2 * td * par
    sib_base = 2 * td * (1 - par)

    def step(s, carry):
        t = tile_at(s)
        far_state(s).wait()
        near[far_base + t] = land[s]
        load_blocks(s).wait()
        moved = mm(blocks[t, 0], near[table[s * slots]])
        for k in range(1, slots):
            moved += mm(blocks[t, k], near[table[s * slots + k]])
        moved = moved.astype(BF16)
        xs[t] = moved
        pre = mm(moved, w_in[...]) + bias[...]
        sig = jax.nn.sigmoid(pre)
        hs[t] = (pre * sig).astype(BF16)
        here = cot[t]
        back = lax.dot_general(here, w_out[...], NT, preferred_element_type=F32)
        pg = (back * sig * (1.0 + pre * (1.0 - sig))).astype(BF16)
        pgs[t] = pg
        up = here.astype(F32) + lax.dot_general(pg, w_in[...], NT, preferred_element_type=F32)
        up_t = jnp.transpose(up).astype(BF16)
        for k in range(slots):
            p = s * slots + k
            sums[p] = mm(up_t, blocks[t, k]) + sums[table[pairs + p]]
        return carry

    lax.fori_loop(0, td, step, 0)

    def far_part(i):
        return send(far_out.at[i], far_in.at[i], cfar_ssem.at[i], cfar_rsem.at[i], far)

    def sib_part(i):
        return send(sib_out.at[i], sib_in.at[i], csib_ssem.at[i], csib_rsem.at[i], sib)

    def post_far(i, carry):
        far_out[i] = sums[table[2 * pairs + far_base + i]].astype(BF16)
        far_part(i).start()
        return carry

    lax.fori_loop(0, td, post_far, 0)

    def post_sib(i, carry):
        sib_out[i] = sums[table[2 * pairs + sib_base + i]].astype(BF16)
        sib_part(i).start()
        return carry

    lax.fori_loop(0, td, post_sib, 0)

    acc[...] = jnp.zeros_like(acc)

    def weights(t, carry):
        acc[0] += lax.dot_general(xs[t], pgs[t], TN, preferred_element_type=F32)
        acc[1] += lax.dot_general(cot[t], hs[t], TN, preferred_element_type=F32)
        return carry

    lax.fori_loop(0, td, weights, 0)

    core_copy = send(acc.at[1 - par], core_in, core_sem.at[0], core_sem.at[1], sib)
    core_copy.start()
    core_copy.wait()
    for z in range(nz):
        rows = pl.ds(z * rz, rz)
        piece = acc[par, rows] + core_in[rows]
        acc[par, rows] = piece
        z_out[z] = piece.astype(BF16)
    z_copies = []
    for d in range(1, nz):
        there = lax.rem(zi + d, nz)
        z_copies.append(
            send(z_out.at[there], z_in.at[d - 1], z_ssem.at[d - 1], z_rsem.at[d - 1], z_mates[d - 1])
        )
        z_copies[-1].start()
    total = acc[par, pl.ds(pl.multiple_of(zi * rz, rz), rz)]
    for d in range(1, nz):
        z_copies[d - 1].wait()
        total += z_in[d - 1].astype(F32)
    y_out[...] = total
    y_copy = send(y_out, y_in, y_sem.at[0], y_sem.at[1], y_mate)
    y_copy.start()
    y_copy.wait()
    gw[par, zi] = (y_out[...] + y_in[...]).astype(BF16)
    g_copies = []
    for d in range(1, nz):
        g_copies.append(
            send(gw.at[par, zi], gw.at[par, zi], g_ssem.at[d - 1], g_rsem.at[d - 1], z_mates[d - 1])
        )
        g_copies[-1].start()
    for g_copy in g_copies:
        g_copy.wait()
    last_copy = send(gw.at[par], gw.at[par], last_sem.at[0], last_sem.at[1], sib)
    last_copy.start()

    def out_copy(i):
        return pltpu.make_async_copy(out_buf.at[i], out_state.at[i], out_sem.at[i])

    def finish(i, carry):
        own = sums[table[2 * pairs + td + i]].astype(BF16).astype(F32)
        sib_part(i).wait()
        far_part(i).wait()
        whole = own + sib_in[i].astype(F32) + far_in[i].astype(F32)
        out_buf[i] = jnp.transpose(whole)
        out_copy(i).start()
        return carry

    lax.fori_loop(0, td, finish, 0)
    last_copy.wait()
    w_copy = pltpu.make_async_copy(gw, out_w, local_sem.at[2])
    w_copy.start()
    for i in range(td):
        out_copy(i).wait()
    w_copy.wait()


def exchange(n, table, state, cotangent, blocks, w_in, bias, w_out):
    td, slots, cols, _ = blocks.shape
    feat = state.shape[2]
    hid = w_in.shape[1]
    nz = n // 4
    rz = feat // nz
    dma = pltpu.SemaphoreType.DMA
    vmem = pl.BlockSpec(memory_space=pltpu.VMEM)
    hbm = pl.BlockSpec(memory_space=pl.ANY)
    return pl.pallas_call(
        functools.partial(kernel, n),
        out_shape=(
            jax.ShapeDtypeStruct((td, cols, feat), F32),
            jax.ShapeDtypeStruct((2, nz, rz, hid), BF16),
        ),
        in_specs=[pl.BlockSpec(memory_space=pltpu.SMEM), hbm, hbm, hbm, vmem, vmem, vmem],
        out_specs=(hbm, hbm),
        scratch_shapes=[
            pltpu.VMEM((3 * td + 1, cols, feat), BF16),
            pltpu.VMEM((td, cols, feat), BF16),
            pltpu.VMEM((td, slots, cols, cols), BF16),
            pltpu.VMEM((td, cols, feat), BF16),
            pltpu.VMEM((td * slots + 1, feat, cols), F32),
            pltpu.VMEM((td, cols, feat), BF16),
            pltpu.VMEM((td, cols, hid), BF16),
            pltpu.VMEM((td, cols, hid), BF16),
            pltpu.VMEM((td, feat, cols), BF16),
            pltpu.VMEM((td, feat, cols), BF16),
            pltpu.VMEM((td, feat, cols), BF16),
            pltpu.VMEM((td, feat, cols), BF16),
            pltpu.VMEM((td, cols, feat), F32),
            pltpu.VMEM((2, feat, hid), F32),
            pltpu.VMEM((feat, hid), F32),
            pltpu.VMEM((nz, rz, hid), BF16),
            pltpu.VMEM((nz - 1, rz, hid), BF16),
            pltpu.VMEM((rz, hid), F32),
            pltpu.VMEM((rz, hid), F32),
            pltpu.VMEM((2, nz, rz, hid), BF16),
            dma((3,)),
            dma((td,)),
            dma((td,)),
            dma((td,)),
            dma((td,)),
            dma,
            dma,
            dma((td,)),
            dma((td,)),
            dma((td,)),
            dma((td,)),
            dma((2,)),
            dma((nz - 1,)),
            dma((nz - 1,)),
            dma((2,)),
            dma((nz - 1,)),
            dma((nz - 1,)),
            dma((2,)),
        ],
        compiler_params=pltpu.CompilerParams(
            collective_id=0, has_side_effects=True, vmem_limit_bytes=56 * 1024 * 1024
        ),
    )(table, state, cotangent, blocks, w_in, bias, w_out)


def per_device(state_field, cotangent, interp_blocks, upstream, src_counts, w_in, in_bias, w_out):
    td, cols, feat = state_field.shape
    slots = upstream.shape[1]
    n = lax.axis_size("cols")
    tile_total = td * n
    pairs = td * slots
    me = lax.axis_index("cols")
    live = jnp.arange(slots)[None, :] < src_counts[:, None]
    local = (upstream - me * td + td) % tile_total
    marked = jnp.where(live, local, -1)
    marked = jnp.where(me % 2 == 0, jnp.flip(marked, 0), marked).reshape(-1)
    order = jnp.arange(pairs, dtype=jnp.int32)
    same = (marked[:, None] == marked[None, :]) & (order[None, :] < order[:, None])
    before = jnp.max(jnp.where(same & (marked[:, None] >= 0), order[None, :], -1), axis=1)
    targets = jnp.arange(3 * td, dtype=jnp.int32)
    last = jnp.max(jnp.where(targets[:, None] == marked[None, :], order[None, :], -1), axis=1)
    table = jnp.concatenate(
        [
            jnp.where(marked < 0, 3 * td, marked),
            jnp.where(before < 0, pairs, before),
            jnp.where(last < 0, pairs, last),
        ]
    ).astype(jnp.int32)
    grad_state, gw = exchange(
        n, table, state_field, cotangent, interp_blocks, w_in, in_bias[None, :], w_out
    )
    norm_scale = 1.0 / jnp.sqrt(F32(tile_total * cols))
    hid = w_in.shape[1]
    grad_w_in = gw[0].reshape(feat, hid).astype(F32) * norm_scale
    grad_w_out = gw[1].reshape(feat, hid).astype(F32).T * norm_scale
    return (grad_state, grad_w_in, grad_w_out)


def solution(mesh):
    placed = (
        P(("groups", "cols"), None, None),
        P(("groups", "cols"), None, None),
        P(("groups", "cols"), None, None, None),
        P(("groups", "cols"), None),
        P(("groups", "cols")),
        P(),
        P(),
        P(),
    )
    return jax.shard_map(
        per_device,
        mesh=mesh,
        in_specs=placed,
        out_specs=(P(("groups", "cols"), None, None), P("groups", None), P("groups", None)),
        check_vma=False,
    )
```

time: 200 us -> 77.4 us (0.39)
  waiting for transfers between devices: 119 us -> 0 us
  Pallas kernels: 0 us -> 69.2 us
  matrix products: 40.5 us -> 0 us
  between operations: 14.2 us -> 0.69 us
  local copies, waits for them, and re-layouts: 12 us -> 2.41 us
  other arithmetic: 9.11 us -> 4.6 us
  starting transfers between devices: 4.47 us -> 0 us
    psum x1 -> x0, waiting for transfers between devices: 95.3 us -> none  [per_device(): grad_w_in, grad_w_out = lax.psum((grad_in_part, grad_out_part), 'cols')]
    pallas_call x0 -> x1, Pallas kernels: none -> 69.2 us  [exchange(): pl.pallas_call(functools.partial(kernel, n), out_shape=(jax.ShapeDtypeStr...]
    dot_general x8 -> x0, matrix products: 40.5 us -> none  [the longest x1 18.2 us: per_device(): jnp.einsum('wp,pdf->wdf', slot_table, products.reshape(tiles_dev * slot_c...]
    ppermute x4 -> x0, waiting for transfers between devices: 23.2 us -> none  [the longest x1 21.7 us: with_halo(): before = lax.ppermute(last, axis, up)]
    gather x1 -> x0, local copies, waits for them, and re-layouts: 5.27 us -> none  [per_device(): upstream_cells = jnp.take(near_tiles, local_slot.reshape(-1), axis=0)]
    ppermute x4 -> x0, starting transfers between devices: 4.43 us -> none  [the longest x1 2.68 us: with_halo(): before = lax.ppermute(last, axis, up)]
    unnamed x23 -> x3, local copies, waits for them, and re-layouts: 5.15 us -> 1.32 us
  transfers between devices with their start and end apart: 5 -> 0, of which waited for: 3 -> 0; matrix products, arithmetic and copies ran while one was open for 3% -> 0% of each run, Pallas kernels for 0% -> 0%
where the time goes in v1:
time: 77.4 us; the launch traced here: 76.9 us
  Pallas kernels  69.2 us (89%)
  other arithmetic  4.6 us (6%)
  local copies, waits for them, and re-layouts  2.41 us (3%)
    pallas_call x1, Pallas kernels, exchange(): pl.pallas_call(functools.partial(kernel, n), out_shape=(jax.ShapeDtypeStr...  69.2 us
    mul x1, other arithmetic, per_device(): grad_w_out = gw[1].reshape(feat, hid).astype(F32).T * norm_scale  2.12 us

profile of v1, /device:TPU:1, one launch (start us, length us, event | category | flops | bytes accessed | tf_op | source)
XLA Modules:
  0.0 76.9 jit_solution(10121333693770198670)
XLA Ops:
  0.6 0.8 fusion.3
  1.4 0.8 broadcast_select_fusion
  2.2 0.1 reshape.25
  2.3 0.1 select_reduce_fusion.1
  2.4 0.2 select_reduce_fusion
  2.6 0.6 pad_add_fusion.table
  3.2 69.2 %shard_map.103 = (f32[8,256,256]{2,1,0:T(8,128)}, bf16[2,4,64,512]{3,2,1,0:T(8,128)(2,1)}) custom-call(s32[136]{0:T(256)} %pad_add_fusion.table, bf16[8,256,256]{2,1,0:T(8,128)(2,1)} %state.1, bf16[8,256,256]{2,1,0:T(8,128)(2,1)} %cot_hbm.1, bf16[8,7,256,256]{3,2,1,0:T(8,128)(2,1)} %blocks_hbm.1, bf16[256,512]{1,0:T(8,128)(2,1)} %w_in.1, f32[1,512]{1,0:T(1,128)} %bitcast.7, ...), custom_call_target="tpu_custom_call" | custom-call | tf_op jit(solution)/shard_map/pallas_call | solution.py:252
  72.5 0.0 copy-start
  72.5 2.1 %convert_multiply_fusion = (f32[1,4,64,512]{3,2,1,0:T(8,128)S(1)}, f32[1,4,64,512]{3,2,1,0:T(8,128)}) fusion(bf16[2,4,64,512]{3,2,1,0:T(8,128)(2,1)} %get-tuple-element.6), kind=kLoop, calls=%fused_computation | loop fusion | flops 524288 | bytes 1572864 | tf_op jit(solution)/shard_map/mul | solution.py:335
  74.6 1.0 %copy.12 = f32[256,512]{0,1:T(8,128)} copy(f32[256,512]{1,0:T(8,128)S(1)} %bitcast.4) | data formatting | bytes 1048576 | tf_op jit(solution)/shard_map/mul | solution.py:335
  75.6 0.0 copy-done
  75.6 1.3 %copy.14 = f32[8,256,256]{2,1,0:T(8,128)} copy(f32[8,256,256]{2,1,0:T(8,128)S(1)} %copy-done) | data formatting | bytes 4194304
  (4 shorter events, 0.0 us)
Async XLA Ops:
  72.5 3.1 %copy-start = (f32[8,256,256]{2,1,0:T(8,128)S(1)}, f32[8,256,256]{2,1,0:T(8,128)}, u32[]{:S(2)}) copy-start(f32[8,256,256]{2,1,0:T(8,128)} %get-tuple-element.14) | copy-start | bytes 6291460

commit v2 on v1

--- a/solution.py
+++ b/solution.py
@@ -28,7 +28,8 @@
     bias,
     w_out,
     out_state,
-    out_w,
+    out_w_in,
+    out_w_out,
     near,
     land,
     blocks,
@@ -49,6 +50,7 @@
     y_out,
     y_in,
     gw,
+    turned,
     local_sem,
     blocks_sem,
     out_sem,
@@ -129,8 +131,19 @@
     far_base = 2 * td * par
     sib_base = 2 * td * (1 - par)
 
+    acc[...] = jnp.zeros_like(acc)
+
+    def weights(t):
+        acc[0] += lax.dot_general(xs[t], pgs[t], TN, preferred_element_type=F32)
+        acc[1] += lax.dot_general(cot[t], hs[t], TN, preferred_element_type=F32)
+
     def step(s, carry):
         t = tile_at(s)
+
+        @pl.when(s > 0)
+        def _():
+            weights(tile_at(s - 1))
+
         far_state(s).wait()
         near[far_base + t] = land[s]
         load_blocks(s).wait()
@@ -166,26 +179,17 @@
         far_part(i).start()
         return carry
 
-    lax.fori_loop(0, td, post_far, 0)
-
     def post_sib(i, carry):
         sib_out[i] = sums[table[2 * pairs + sib_base + i]].astype(BF16)
         sib_part(i).start()
         return carry
 
-    lax.fori_loop(0, td, post_sib, 0)
-
-    acc[...] = jnp.zeros_like(acc)
-
-    def weights(t, carry):
-        acc[0] += lax.dot_general(xs[t], pgs[t], TN, preferred_element_type=F32)
-        acc[1] += lax.dot_general(cot[t], hs[t], TN, preferred_element_type=F32)
-        return carry
-
-    lax.fori_loop(0, td, weights, 0)
-
+    cuts = [0, td // 4, td // 2, td // 2 + td // 8, td - td // 4, td]
+    lax.fori_loop(cuts[0], cuts[1], post_far, 0)
+    weights(tile_at(td - 1))
     core_copy = send(acc.at[1 - par], core_in, core_sem.at[0], core_sem.at[1], sib)
     core_copy.start()
+    lax.fori_loop(0, td, post_sib, 0)
     core_copy.wait()
     for z in range(nz):
         rows = pl.ds(z * rz, rz)
@@ -199,25 +203,29 @@
             send(z_out.at[there], z_in.at[d - 1], z_ssem.at[d - 1], z_rsem.at[d - 1], z_mates[d - 1])
         )
         z_copies[-1].start()
+    lax.fori_loop(cuts[1], cuts[2], post_far, 0)
     total = acc[par, pl.ds(pl.multiple_of(zi * rz, rz), rz)]
     for d in range(1, nz):
         z_copies[d - 1].wait()
         total += z_in[d - 1].astype(F32)
-    y_out[...] = total
+    y_out[...] = total.astype(BF16)
     y_copy = send(y_out, y_in, y_sem.at[0], y_sem.at[1], y_mate)
     y_copy.start()
+    lax.fori_loop(cuts[2], cuts[3], post_far, 0)
     y_copy.wait()
-    gw[par, zi] = (y_out[...] + y_in[...]).astype(BF16)
+    gw[par, zi] = (y_out[...].astype(F32) + y_in[...].astype(F32)).astype(BF16)
     g_copies = []
     for d in range(1, nz):
         g_copies.append(
             send(gw.at[par, zi], gw.at[par, zi], g_ssem.at[d - 1], g_rsem.at[d - 1], z_mates[d - 1])
         )
         g_copies[-1].start()
+    lax.fori_loop(cuts[3], cuts[4], post_far, 0)
     for g_copy in g_copies:
         g_copy.wait()
     last_copy = send(gw.at[par], gw.at[par], last_sem.at[0], last_sem.at[1], sib)
     last_copy.start()
+    lax.fori_loop(cuts[4], cuts[5], post_far, 0)
 
     def out_copy(i):
         return pltpu.make_async_copy(out_buf.at[i], out_state.at[i], out_sem.at[i])
@@ -233,11 +241,16 @@
 
     lax.fori_loop(0, td, finish, 0)
     last_copy.wait()
-    w_copy = pltpu.make_async_copy(gw, out_w, local_sem.at[2])
-    w_copy.start()
+    feat, hid = w_in.shape
+    w_in_copy = pltpu.make_async_copy(gw.at[0], out_w_in, local_sem.at[2])
+    w_in_copy.start()
+    turned[...] = jnp.transpose(gw[1].reshape(feat, hid).astype(F32)).astype(BF16)
+    w_out_copy = pltpu.make_async_copy(turned, out_w_out, local_sem.at[0])
+    w_out_copy.start()
     for i in range(td):
         out_copy(i).wait()
-    w_copy.wait()
+    w_in_copy.wait()
+    w_out_copy.wait()
 
 
 def exchange(n, table, state, cotangent, blocks, w_in, bias, w_out):
@@ -253,10 +266,11 @@
         functools.partial(kernel, n),
         out_shape=(
             jax.ShapeDtypeStruct((td, cols, feat), F32),
-            jax.ShapeDtypeStruct((2, nz, rz, hid), BF16),
+            jax.ShapeDtypeStruct((nz, rz, hid), BF16),
+            jax.ShapeDtypeStruct((hid, feat), BF16),
         ),
         in_specs=[pl.BlockSpec(memory_space=pltpu.SMEM), hbm, hbm, hbm, vmem, vmem, vmem],
-        out_specs=(hbm, hbm),
+        out_specs=(hbm, hbm, hbm),
         scratch_shapes=[
             pltpu.VMEM((3 * td + 1, cols, feat), BF16),
             pltpu.VMEM((td, cols, feat), BF16),
@@ -275,9 +289,10 @@
             pltpu.VMEM((feat, hid), F32),
             pltpu.VMEM((nz, rz, hid), BF16),
             pltpu.VMEM((nz - 1, rz, hid), BF16),
-            pltpu.VMEM((rz, hid), F32),
-            pltpu.VMEM((rz, hid), F32),
+            pltpu.VMEM((rz, hid), BF16),
+            pltpu.VMEM((rz, hid), BF16),
             pltpu.VMEM((2, nz, rz, hid), BF16),
+            pltpu.VMEM((hid, feat), BF16),
             dma((3,)),
             dma((td,)),
             dma((td,)),
@@ -326,13 +341,13 @@
             jnp.where(last < 0, pairs, last),
         ]
     ).astype(jnp.int32)
-    grad_state, gw = exchange(
+    grad_state, gw_in, gw_out = exchange(
         n, table, state_field, cotangent, interp_blocks, w_in, in_bias[None, :], w_out
     )
     norm_scale = 1.0 / jnp.sqrt(F32(tile_total * cols))
     hid = w_in.shape[1]
-    grad_w_in = gw[0].reshape(feat, hid).astype(F32) * norm_scale
-    grad_w_out = gw[1].reshape(feat, hid).astype(F32).T * norm_scale
+    grad_w_in = gw_in.reshape(feat, hid).astype(F32) * norm_scale
+    grad_w_out = gw_out.astype(F32) * norm_scale
     return (grad_state, grad_w_in, grad_w_out)
 
 

time: 77.4 us -> 78.1 us (level)
  other arithmetic: 4.6 us -> 6.08 us
  Pallas kernels: 69.2 us -> 67.9 us
    unnamed x3 -> x1, local copies, waits for them, and re-layouts: 1.32 us -> 3.04 us
    mul x1 -> x2, other arithmetic: 2.12 us -> 3.6 us  [the longest x1 1.81 us: per_device(): grad_w_in = gw_in.reshape(feat, hid).astype(F32) * norm_scale]
    pallas_call x1, Pallas kernels: 69.2 us -> 67.9 us  [exchange(): pl.pallas_call(functools.partial(kernel, n), out_shape=(jax.ShapeDtypeStr...]
    mul x1 -> x0, local copies, waits for them, and re-layouts: 0.99 us -> none  [per_device(): grad_w_out = gw[1].reshape(feat, hid).astype(F32).T * norm_scale]
where the time goes in v2:
time: 78.1 us; the launch traced here: 77.8 us
  Pallas kernels  67.9 us (87%)
  other arithmetic  6.08 us (8%)
  local copies, waits for them, and re-layouts  3.13 us (4%)
    pallas_call x1, Pallas kernels, exchange(): pl.pallas_call(functools.partial(kernel, n), out_shape=(jax.ShapeDtypeStr...  67.9 us
    unnamed x1, local copies, waits for them, and re-layouts  3.04 us
    mul x1, other arithmetic, per_device(): grad_w_in = gw_in.reshape(feat, hid).astype(F32) * norm_scale  1.81 us
    mul x1, other arithmetic, per_device(): grad_w_out = gw_out.astype(F32) * norm_scale  1.79 us

profile of v2, /device:TPU:1, one launch (start us, length us, event | category | flops | bytes accessed | tf_op | source)
XLA Modules:
  0.0 77.8 jit_solution(260051233737264011)
XLA Ops:
  0.6 0.8 fusion.3
  1.4 0.8 broadcast_select_fusion
  2.2 0.1 reshape.23
  2.3 0.1 select_reduce_fusion.1
  2.4 0.2 select_reduce_fusion
  2.6 0.6 pad_add_fusion.table
  3.2 67.9 %shard_map.103 = (f32[8,256,256]{2,1,0:T(8,128)}, bf16[4,64,512]{2,1,0:T(8,128)(2,1)}, bf16[512,256]{1,0:T(8,128)(2,1)}) custom-call(s32[136]{0:T(256)} %pad_add_fusion.table, bf16[8,256,256]{2,1,0:T(8,128)(2,1)} %state.1, bf16[8,256,256]{2,1,0:T(8,128)(2,1)} %cot_hbm.1, bf16[8,7,256,256]{3,2,1,0:T(8,128)(2,1)} %blocks_hbm.1, bf16[256,512]{1,0:T(8,128)(2,1)} %w_in.1, ...), custom_call_target="tpu_custom_call" | custom-call | tf_op jit(solution)/shard_map/pallas_call | solution.py:265
  71.1 1.8 %convert_multiply_fusion.1 = f32[4,64,512]{2,1,0:T(8,128)} fusion(bf16[4,64,512]{2,1,0:T(8,128)(2,1)} %get-tuple-element.7), kind=kLoop, calls=%fused_computation.1 | loop fusion | flops 262144 | bytes 786432 | tf_op jit(solution)/shard_map/mul | solution.py:349
  72.9 1.8 %convert_multiply_fusion = f32[512,256]{1,0:T(8,128)} fusion(bf16[512,256]{1,0:T(8,128)(2,1)} %get-tuple-element.8), kind=kLoop, calls=%fused_computation | loop fusion | flops 262144 | bytes 786432 | tf_op jit(solution)/shard_map/mul | solution.py:350
  74.7 3.0 %copy.12 = f32[8,256,256]{2,1,0:T(8,128)} copy(f32[8,256,256]{2,1,0:T(8,128)} %get-tuple-element.14) | data formatting | bytes 4194304
  (4 shorter events, 0.0 us)

commit v3 on v2

--- a/solution.py
+++ b/solution.py
@@ -1,4 +1,5 @@
 import functools
+import math
 
 import jax
 import jax.numpy as jnp
@@ -69,6 +70,7 @@
     g_ssem,
     g_rsem,
     last_sem,
+    turn_sem,
 ):
     td, slots = blocks.shape[0], blocks.shape[1]
     nz = z_out.shape[0]
@@ -78,6 +80,7 @@
     par = lax.rem(me, 2)
     sib = me + 1 - 2 * par
     far = lax.rem(me - 1 + 2 * par + n, n)
+    norm_scale = 1.0 / math.sqrt(n * td * blocks.shape[2])
     zi = me // 4
     low = lax.rem(me, 4)
     y_mate = me + 2 - 4 * (low // 2)
@@ -146,6 +149,11 @@
 
         far_state(s).wait()
         near[far_base + t] = land[s]
+
+        @pl.when(s == td - 1)
+        def _():
+            pl.semaphore_signal(turn_sem, inc=1, device_id={"cols": sib}, device_id_type=MESH)
+
         load_blocks(s).wait()
         moved = mm(blocks[t, 0], near[table[s * slots]])
         for k in range(1, slots):
@@ -184,7 +192,10 @@
         sib_part(i).start()
         return carry
 
-    cuts = [0, td // 4, td // 2, td // 2 + td // 8, td - td // 4, td]
+    direct = lax.rem((low + 1) // 2, 2)
+    most, more = td // 2 + td // 8, td - td // 8
+    cuts = [0, td // 8, td // 4, td - (td - most) * direct, td - (td - more) * direct, td]
+    pl.semaphore_wait(turn_sem, 1)
     lax.fori_loop(cuts[0], cuts[1], post_far, 0)
     weights(tile_at(td - 1))
     core_copy = send(acc.at[1 - par], core_in, core_sem.at[0], core_sem.at[1], sib)
@@ -242,9 +253,10 @@
     lax.fori_loop(0, td, finish, 0)
     last_copy.wait()
     feat, hid = w_in.shape
-    w_in_copy = pltpu.make_async_copy(gw.at[0], out_w_in, local_sem.at[2])
+    acc[0] = gw[0].reshape(feat, hid).astype(F32) * norm_scale
+    w_in_copy = pltpu.make_async_copy(acc.at[0], out_w_in, local_sem.at[2])
     w_in_copy.start()
-    turned[...] = jnp.transpose(gw[1].reshape(feat, hid).astype(F32)).astype(BF16)
+    turned[...] = jnp.transpose(gw[1].reshape(feat, hid).astype(F32) * norm_scale)
     w_out_copy = pltpu.make_async_copy(turned, out_w_out, local_sem.at[0])
     w_out_copy.start()
     for i in range(td):
@@ -266,8 +278,8 @@
         functools.partial(kernel, n),
         out_shape=(
             jax.ShapeDtypeStruct((td, cols, feat), F32),
-            jax.ShapeDtypeStruct((nz, rz, hid), BF16),
-            jax.ShapeDtypeStruct((hid, feat), BF16),
+            jax.ShapeDtypeStruct((feat, hid), F32),
+            jax.ShapeDtypeStruct((hid, feat), F32),
         ),
         in_specs=[pl.BlockSpec(memory_space=pltpu.SMEM), hbm, hbm, hbm, vmem, vmem, vmem],
         out_specs=(hbm, hbm, hbm),
@@ -292,7 +304,7 @@
             pltpu.VMEM((rz, hid), BF16),
             pltpu.VMEM((rz, hid), BF16),
             pltpu.VMEM((2, nz, rz, hid), BF16),
-            pltpu.VMEM((hid, feat), BF16),
+            pltpu.VMEM((hid, feat), F32),
             dma((3,)),
             dma((td,)),
             dma((td,)),
@@ -311,6 +323,7 @@
             dma((nz - 1,)),
             dma((nz - 1,)),
             dma((2,)),
+            pltpu.SemaphoreType.REGULAR,
         ],
         compiler_params=pltpu.CompilerParams(
             collective_id=0, has_side_effects=True, vmem_limit_bytes=56 * 1024 * 1024
@@ -341,14 +354,9 @@
             jnp.where(last < 0, pairs, last),
         ]
     ).astype(jnp.int32)
-    grad_state, gw_in, gw_out = exchange(
+    return exchange(
         n, table, state_field, cotangent, interp_blocks, w_in, in_bias[None, :], w_out
     )
-    norm_scale = 1.0 / jnp.sqrt(F32(tile_total * cols))
-    hid = w_in.shape[1]
-    grad_w_in = gw_in.reshape(feat, hid).astype(F32) * norm_scale
-    grad_w_out = gw_out.astype(F32) * norm_scale
-    return (grad_state, grad_w_in, grad_w_out)
 
 
 def solution(mesh):

time: 78.1 us -> 74 us (0.948)
  other arithmetic: 6.08 us -> 2.48 us
  Pallas kernels: 67.9 us -> 65.7 us
  local copies, waits for them, and re-layouts: 3.13 us -> 4.82 us
    mul x2 -> x0, other arithmetic: 3.6 us -> none  [the longest x1 1.81 us: per_device(): grad_w_in = gw_in.reshape(feat, hid).astype(F32) * norm_scale]
    pallas_call x1, Pallas kernels: 67.9 us -> 65.7 us  [exchange(): pl.pallas_call(functools.partial(kernel, n), out_shape=(jax.ShapeDtypeStr...]
    unnamed x1 -> x7, local copies, waits for them, and re-layouts: 3.04 us -> 4.73 us
where the time goes in v3:
time: 74 us; the launch traced here: 73.7 us
  Pallas kernels  65.7 us (89%)
  local copies, waits for them, and re-layouts  4.82 us (7%)
  other arithmetic  2.48 us (3%)
    pallas_call x1, Pallas kernels, exchange(): pl.pallas_call(functools.partial(kernel, n), out_shape=(jax.ShapeDtypeStr...  65.7 us
    unnamed x7, local copies, waits for them, and re-layouts  4.73 us

profile of v3, /device:TPU:1, one launch (start us, length us, event | category | flops | bytes accessed | tf_op | source)
XLA Modules:
  0.0 73.7 jit_solution(4908848735145088763)
XLA Ops:
  0.6 0.8 %fusion.3 = s32[8,7]{1,0:T(8,128)S(1)} fusion(s32[8,7]{1,0:T(8,128)} %param.11, s32[]{:T(128)S(6)} %mul.3, s32[8]{0:T(128)} %param.12), kind=kLoop, calls=%fused_computation.10 | loop fusion | flops 840 | bytes 484 | tf_op jit(solution)/shard_map/jit(_where)/select_n | solution.py:343
  1.4 0.8 %broadcast_select_fusion = s32[8,7]{1,0:T(8,128)S(1)} fusion(s32[8,7]{1,0:T(8,128)S(1)} %rev.4, pred[]{:T(512)S(6)} %eq.18, s32[8,7]{1,0:T(8,128)} %param.11, s32[]{:T(128)S(6)} %mul.3, s32[8]{0:T(128)} %param.12), kind=kLoop, calls=%fused_computation.15 | loop fusion | flops 896 | bytes 709 | tf_op jit(solution)/shard_map/jit(_where)/select_n | solution.py:344
  2.2 0.1 reshape.19
  2.3 0.1 select_reduce_fusion.1
  2.4 0.2 select_reduce_fusion
  2.6 0.6 pad_add_fusion.table
  3.2 65.7 %shard_map.103 = (f32[8,256,256]{2,1,0:T(8,128)}, f32[256,512]{1,0:T(8,128)}, f32[512,256]{1,0:T(8,128)}) custom-call(s32[136]{0:T(256)} %pad_add_fusion.table, bf16[8,256,256]{2,1,0:T(8,128)(2,1)} %state.1, bf16[8,256,256]{2,1,0:T(8,128)(2,1)} %cot_hbm.1, bf16[8,7,256,256]{3,2,1,0:T(8,128)(2,1)} %blocks_hbm.1, bf16[256,512]{1,0:T(8,128)(2,1)} %w_in.1, ...), custom_call_target="tpu_custom_call" | custom-call | tf_op jit(solution)/shard_map/pallas_call | solution.py:277
  69.0 0.0 copy-start.1
  69.0 0.0 copy-start
  69.0 3.1 %copy.14 = f32[8,256,256]{2,1,0:T(8,128)} copy(f32[8,256,256]{2,1,0:T(8,128)} %get-tuple-element.8) | data formatting | bytes 4194304
  72.1 0.0 copy-done.1
  72.1 0.8 %copy.15 = f32[256,512]{1,0:T(8,128)} copy(f32[256,512]{1,0:T(8,128)S(1)} %copy-done.1) | data formatting | bytes 1048576
  72.9 0.0 copy-done
  72.9 0.8 %copy.16 = f32[512,256]{1,0:T(8,128)} copy(f32[512,256]{1,0:T(8,128)S(1)} %copy-done) | data formatting | bytes 1048576
  (4 shorter events, 0.0 us)
Async XLA Ops:
  69.0 3.2 %copy-start.1 = (f32[256,512]{1,0:T(8,128)S(1)}, f32[256,512]{1,0:T(8,128)}, u32[]{:S(2)}) copy-start(f32[256,512]{1,0:T(8,128)} %get-tuple-element.9) | copy-start | bytes 1572868
  69.0 3.9 %copy-start = (f32[512,256]{1,0:T(8,128)S(1)}, f32[512,256]{1,0:T(8,128)}, u32[]{:S(2)}) copy-start(f32[512,256]{1,0:T(8,128)} %get-tuple-element.10) | copy-start | bytes 1572868

commit v4 on v3

--- a/solution.py
+++ b/solution.py
@@ -193,8 +193,8 @@
         return carry
 
     direct = lax.rem((low + 1) // 2, 2)
-    most, more = td // 2 + td // 8, td - td // 8
-    cuts = [0, td // 8, td // 4, td - (td - most) * direct, td - (td - more) * direct, td]
+    most = td // 2 + td // 8
+    cuts = [0, td // 8, td // 4, td - (td - most) * direct]
     pl.semaphore_wait(turn_sem, 1)
     lax.fori_loop(cuts[0], cuts[1], post_far, 0)
     weights(tile_at(td - 1))
@@ -231,12 +231,7 @@
             send(gw.at[par, zi], gw.at[par, zi], g_ssem.at[d - 1], g_rsem.at[d - 1], z_mates[d - 1])
         )
         g_copies[-1].start()
-    lax.fori_loop(cuts[3], cuts[4], post_far, 0)
-    for g_copy in g_copies:
-        g_copy.wait()
-    last_copy = send(gw.at[par], gw.at[par], last_sem.at[0], last_sem.at[1], sib)
-    last_copy.start()
-    lax.fori_loop(cuts[4], cuts[5], post_far, 0)
+    lax.fori_loop(cuts[3], td, post_far, 0)
 
     def out_copy(i):
         return pltpu.make_async_copy(out_buf.at[i], out_state.at[i], out_sem.at[i])
@@ -250,7 +245,12 @@
         out_copy(i).start()
         return carry
 
-    lax.fori_loop(0, td, finish, 0)
+    lax.fori_loop(0, td // 2, finish, 0)
+    for g_copy in g_copies:
+        g_copy.wait()
+    last_copy = send(gw.at[par], gw.at[par], last_sem.at[0], last_sem.at[1], sib)
+    last_copy.start()
+    lax.fori_loop(td // 2, td, finish, 0)
     last_copy.wait()
     feat, hid = w_in.shape
     acc[0] = gw[0].reshape(feat, hid).astype(F32) * norm_scale

time: 74 us -> 73.8 us (level)
  no operation moved by 1% of the time
where the time goes in v4:
time: 73.8 us; the launch traced here: 73.5 us
  Pallas kernels  65.5 us (89%)
  local copies, waits for them, and re-layouts  4.82 us (7%)
  other arithmetic  2.48 us (3%)
    pallas_call x1, Pallas kernels, exchange(): pl.pallas_call(functools.partial(kernel, n), out_shape=(jax.ShapeDtypeStr...  65.5 us
    unnamed x7, local copies, waits for them, and re-layouts  4.73 us

profile of v4, /device:TPU:1, one launch (start us, length us, event | category | flops | bytes accessed | tf_op | source)
XLA Modules:
  0.0 73.5 jit_solution(13876756395131447464)
XLA Ops:
  0.6 0.8 %fusion.3 = s32[8,7]{1,0:T(8,128)S(1)} fusion(s32[8,7]{1,0:T(8,128)} %param.11, s32[]{:T(128)S(6)} %mul.3, s32[8]{0:T(128)} %param.12), kind=kLoop, calls=%fused_computation.10 | loop fusion | flops 840 | bytes 484 | tf_op jit(solution)/shard_map/jit(_where)/select_n | solution.py:343
  1.4 0.8 %broadcast_select_fusion = s32[8,7]{1,0:T(8,128)S(1)} fusion(s32[8,7]{1,0:T(8,128)S(1)} %rev.4, pred[]{:T(512)S(6)} %eq.18, s32[8,7]{1,0:T(8,128)} %param.11, s32[]{:T(128)S(6)} %mul.3, s32[8]{0:T(128)} %param.12), kind=kLoop, calls=%fused_computation.15 | loop fusion | flops 896 | bytes 709 | tf_op jit(solution)/shard_map/jit(_where)/select_n | solution.py:344
  2.2 0.1 reshape.19
  2.3 0.1 select_reduce_fusion.1
  2.4 0.2 select_reduce_fusion
  2.6 0.6 pad_add_fusion.table
  3.2 65.5 %shard_map.103 = (f32[8,256,256]{2,1,0:T(8,128)}, f32[256,512]{1,0:T(8,128)}, f32[512,256]{1,0:T(8,128)}) custom-call(s32[136]{0:T(256)} %pad_add_fusion.table, bf16[8,256,256]{2,1,0:T(8,128)(2,1)} %state.1, bf16[8,256,256]{2,1,0:T(8,128)(2,1)} %cot_hbm.1, bf16[8,7,256,256]{3,2,1,0:T(8,128)(2,1)} %blocks_hbm.1, bf16[256,512]{1,0:T(8,128)(2,1)} %w_in.1, ...), custom_call_target="tpu_custom_call" | custom-call | tf_op jit(solution)/shard_map/pallas_call | solution.py:277
  68.8 0.0 copy-start.1
  68.8 0.0 copy-start
  68.8 3.1 %copy.14 = f32[8,256,256]{2,1,0:T(8,128)} copy(f32[8,256,256]{2,1,0:T(8,128)} %get-tuple-element.8) | data formatting | bytes 4194304
  71.9 0.0 copy-done.1
  72.0 0.8 %copy.15 = f32[256,512]{1,0:T(8,128)} copy(f32[256,512]{1,0:T(8,128)S(1)} %copy-done.1) | data formatting | bytes 1048576
  72.7 0.0 copy-done
  72.7 0.8 %copy.16 = f32[512,256]{1,0:T(8,128)} copy(f32[512,256]{1,0:T(8,128)S(1)} %copy-done) | data formatting | bytes 1048576
  (4 shorter events, 0.0 us)
Async XLA Ops:
  68.8 3.2 %copy-start.1 = (f32[256,512]{1,0:T(8,128)S(1)}, f32[256,512]{1,0:T(8,128)}, u32[]{:S(2)}) copy-start(f32[256,512]{1,0:T(8,128)} %get-tuple-element.9) | copy-start | bytes 1572868
  68.8 3.9 %copy-start = (f32[512,256]{1,0:T(8,128)S(1)}, f32[512,256]{1,0:T(8,128)}, u32[]{:S(2)}) copy-start(f32[512,256]{1,0:T(8,128)} %get-tuple-element.10) | copy-start | bytes 1572868
